TPU v7x, 32 devices: a whole 2x2x4 slice. The times are simulated.
32 devices in a mesh: grp: 2 (over x), blk: 16 (over z, y, core).
Axes of the slice: x: 2, y: 2, z: 4, core: 2. Of those that a mesh axis runs over, the one named last changes fastest.
Arguments:
- features: bfloat16 [16384, 256], P(('grp', 'blk')), parts along dimension 0, may hold values from -6 to 6
- tile_rows: int32 [512], P(('grp', 'blk')), parts along dimension 0, may hold values from 0 to 63, as said below
- tile_cols: int32 [512], P(('grp', 'blk')), parts along dimension 0, may hold values from 0 to 63, as said below
- tile_live: int32 [32], P(('grp', 'blk')), parts along dimension 0, may hold values from 4 to 16, as said below
- tile_vals: bfloat16 [512, 128, 128], P(('grp', 'blk')), parts along dimension 0, may hold values from -1 to 1
- w_msg: bfloat16 [3, 256, 256], replicated, may hold values from -0.375 to 0.375
- w_self: bfloat16 [3, 256, 256], replicated, may hold values from -0.375 to 0.375
- w_dec: bfloat16 [256, 128], replicated, may hold values from -0.375 to 0.375
- w_head: float32 [128], replicated, may hold values from -0.5 to 0.5
- sample_pairs: int32 [65536, 2], P(('grp', 'blk')), parts along dimension 0, may hold values from 0 to 8191
- targets: float32 [16384], P(('grp', 'blk')), parts along dimension 0, may hold values from -12 to 12
Outputs:
- objective: float32 [2], P('grp'), parts along dimension 0
- grad_msg: float32 [6, 256, 256], P('grp', 'blk'), parts along dimension 0
- grad_self: float32 [6, 256, 256], P('grp', 'blk'), parts along dimension 0
- grad_dec: float32 [512, 128], P(('grp', 'blk')), parts along dimension 0
- grad_head: float32 [256], P('grp'), parts along dimension 0
- grad_input: float32 [16384, 256], P(('grp', 'blk')), parts along dimension 0
There are 2 independent parts, one for each index of `grp`. A program takes and returns all parts, laid end to end along the dimension named above; an argument that names none is the same for every part. Nothing has to cross between parts.
Inputs may be any that keep to these rules, and one draw needn't show every extreme that they name: `tile_rows`: slot s of device d (slots d * 16 to (d + 1) * 16 - 1) lies in one of that device's row blocks d * 4 to (d + 1) * 4 - 1. `tile_cols`: every slot's column block lies at most 2 blocks from its row block around the cycle of 64 blocks, at that distance in both directions on some slots. `tile_live`: live slots come first on each device; some device has all 16 slots live.
All inputs are finite; a program needn't handle non-finite values.
Results may differ from a plain program's by a relative error of at most 0.015.
Values may be sent and summed in bfloat16 or wider, within the bound.
A program may use at most 64 MiB of HBM per device.

v0:
```python
import jax
import jax.numpy as jnp
from jax import lax
from jax.sharding import PartitionSpec as P

LAYERS = 3
HB = 2


norm_eps = 1e-05


def padded(cells, sides, width):
    for axis, dim in sides:
        count = lax.axis_size(axis)
        head = lax.slice_in_dim(cells, 0, width, axis=dim)
        tail = lax.slice_in_dim(cells, cells.shape[dim] - width, cells.shape[dim], axis=dim)
        cells = jnp.concatenate(
            [
                lax.ppermute(tail, axis, [(i, (i + 1) % count) for i in range(count)]),
                cells,
                lax.ppermute(head, axis, [((i + 1) % count, i) for i in range(count)]),
            ],
            axis=dim,
        )
    return cells


def passed_along(array, axis, by):
    size = lax.axis_size(axis)
    return lax.ppermute(array, axis, [(i, (i + by) % size) for i in range(size)])


def silu_slope(values):
    squash = jax.nn.sigmoid(values)
    return squash * (1.0 + values * (1.0 - squash))


def shards(
    features,
    tile_rows,
    tile_cols,
    tile_live,
    tile_vals,
    w_msg,
    w_self,
    w_dec,
    w_head,
    sample_pairs,
    targets,
):
    row_count, feat_width = features.shape
    tile_size = tile_vals.shape[1]
    slot_count = tile_vals.shape[0]
    per_device = row_count // tile_size
    cycle_size = lax.axis_size("blk")
    cycle_pos = lax.axis_index("blk")
    block_total = per_device * cycle_size
    local_row = tile_rows - cycle_pos * per_device
    offsets = (tile_cols - tile_rows + HB) % block_total - HB
    ext_col = local_row + offsets + HB
    live_count = tile_live[0]
    flags = (jnp.arange(slot_count, dtype=jnp.int32) < live_count).astype(jnp.float32)
    ext_blocks = per_device + 2 * HB
    row_hot = (local_row[:, None] == jnp.arange(per_device, dtype=jnp.int32)[None, :]).astype(
        jnp.float32
    )
    ext_hot = (ext_col[:, None] == jnp.arange(ext_blocks, dtype=jnp.int32)[None, :]).astype(
        jnp.float32
    )

    def tile_products(source_blocks, read_index, write_hot, transpose):
        picked = jnp.take(source_blocks, read_index, axis=0)
        form = "tji,tjh->tih" if transpose else "tij,tjh->tih"
        terms = (
            jnp.einsum(form, tile_vals, picked, preferred_element_type=jnp.float32)
            * flags[:, None, None]
        )
        return jnp.einsum("te,tih->eih", write_hot, terms, precision=lax.Precision.HIGHEST)

    hidden = features
    saved = []
    summed = jnp.zeros((row_count, feat_width), jnp.float32)
    for layer in range(LAYERS):
        extended = padded(hidden, (("blk", 0),), HB * tile_size)
        forward_source_blocks = extended.reshape(ext_blocks, tile_size, feat_width)
        forward_total = tile_products(forward_source_blocks, ext_col, row_hot, False)
        message = forward_total.reshape(row_count, feat_width).astype(jnp.bfloat16)
        mixed = jnp.dot(message, w_msg[layer], preferred_element_type=jnp.float32) + jnp.dot(
            hidden, w_self[layer], preferred_element_type=jnp.float32
        )
        update = hidden.astype(jnp.float32) + jax.nn.silu(mixed)
        inv_rms = lax.rsqrt(jnp.mean(update * update, axis=-1, keepdims=True) + norm_eps)
        saved.append((hidden, message, mixed, update, inv_rms))
        hidden = (update * inv_rms).astype(jnp.bfloat16)
        summed = summed + hidden.astype(jnp.float32)
    pooled = summed.astype(jnp.bfloat16)
    pre_head = jnp.dot(pooled, w_dec, preferred_element_type=jnp.float32)
    activ = jax.nn.silu(pre_head)
    scores = jnp.dot(activ, w_head, precision=lax.Precision.HIGHEST)
    all_scores, all_targets = (
        lax.all_gather(scores, "blk", axis=0, tiled=True),
        lax.all_gather(targets, "blk", axis=0, tiled=True),
    )
    first = sample_pairs[:, 0]
    second = sample_pairs[:, 1]
    pair_total = sample_pairs.shape[0]
    margin = all_scores[first] - all_scores[second]
    wanted = jax.nn.sigmoid(all_targets[first] - all_targets[second])
    objective_part = jnp.sum(jax.nn.softplus(margin) - wanted * margin) / pair_total
    d_margin = (jax.nn.sigmoid(margin) - wanted) / pair_total
    node_total = row_count * cycle_size
    d_global = (
        jnp.zeros((node_total,), jnp.float32).at[first].add(d_margin).at[second].add(-d_margin)
    )
    d_scores = lax.psum_scatter(d_global, "blk", scatter_dimension=0, tiled=True)
    d_pre = (d_scores[:, None] * w_head[None, :] * silu_slope(pre_head)).astype(jnp.bfloat16)
    dec_part = jnp.dot(pooled.T, d_pre, preferred_element_type=jnp.float32)
    head_part = jnp.dot(activ.T, d_scores, precision=lax.Precision.HIGHEST)
    d_pooled = jnp.dot(d_pre, w_dec.T, preferred_element_type=jnp.float32)
    grad_dec = lax.psum_scatter(dec_part, "blk", scatter_dimension=0, tiled=True)
    carried = d_pooled
    msg_parts = [None] * LAYERS
    self_parts = [None] * LAYERS
    for layer in reversed(range(LAYERS)):
        hidden, message, mixed, update, inv_rms = saved[layer]
        cubed = inv_rms * inv_rms * inv_rms
        d_update = inv_rms * carried - update * cubed * jnp.mean(
            carried * update, axis=-1, keepdims=True
        )
        d_mixed = (d_update * silu_slope(mixed)).astype(jnp.bfloat16)
        msg_term = jnp.dot(message.T, d_mixed, preferred_element_type=jnp.float32)
        self_term = jnp.dot(hidden.T, d_mixed, preferred_element_type=jnp.float32)
        msg_parts[layer], self_parts[layer] = (
            lax.psum_scatter(msg_term, "blk", scatter_dimension=0, tiled=True),
            lax.psum_scatter(self_term, "blk", scatter_dimension=0, tiled=True),
        )
        d_message = jnp.dot(d_mixed, w_msg[layer].T, preferred_element_type=jnp.float32).astype(
            jnp.bfloat16
        )
        d_hidden = d_update + jnp.dot(d_mixed, w_self[layer].T, preferred_element_type=jnp.float32)
        backward_source_blocks = d_message.reshape(per_device, tile_size, feat_width)
        total = tile_products(backward_source_blocks, local_row, ext_hot, True)
        upper_rim = total[:HB]
        lower_rim = total[HB + per_device :]
        centre = total[HB : HB + per_device]
        from_below = passed_along(lower_rim.astype(jnp.bfloat16), "blk", 1).astype(lower_rim.dtype)
        from_above = passed_along(upper_rim.astype(jnp.bfloat16), "blk", -1).astype(upper_rim.dtype)
        centre = centre.at[:HB].add(from_below)
        centre = centre.at[per_device - HB :].add(from_above)
        d_hidden = d_hidden + centre.reshape(row_count, feat_width)
        if layer > 0:
            carried = d_hidden + d_pooled
        else:
            carried = d_hidden
    grad_msg = jnp.stack(msg_parts)
    grad_self = jnp.stack(self_parts)
    objective, grad_head = lax.psum((objective_part.reshape(1), head_part), "blk")
    return (objective, grad_msg, grad_self, grad_dec, grad_head, carried)


def solution(mesh):
    in_specs = (
        P(("grp", "blk"), None),
        P(("grp", "blk")),
        P(("grp", "blk")),
        P(("grp", "blk")),
        P(("grp", "blk"), None, None),
        P(),
        P(),
        P(),
        P(),
        P(("grp", "blk"), None),
        P(("grp", "blk")),
    )
    out_specs = (
        P("grp"),
        P("grp", "blk", None),
        P("grp", "blk", None),
        P(("grp", "blk"), None),
        P("grp"),
        P(("grp", "blk"), None),
    )
    return jax.shard_map(shards, mesh=mesh, in_specs=in_specs, out_specs=out_specs, check_vma=False)
```

profile of v0, /device:TPU:0, one launch (start us, length us, event | category | flops | bytes accessed | tf_op | source)
XLA Modules:
  0.0 659.8 jit_solution(14464622130148785085)
XLA Ops:
  8.8 5.1 collective-permute-start.1
  29.0 4.4 collective-permute-start.3
  45.5 4.5 collective-permute-start.5
  50.0 17.9 %all-gather.1 = f32[16,1,512]{2,1,0:T(1,128)S(1)} all-gather(f32[1,1,512]{2,1,0:T(1,128)S(1)} %bitcast.204), channel_id=1, replica_groups=mesh['grp'=2,'blk'=16] {'blk'}, dimensions={0}, use_global_device_ids=true | all-gather | bytes 34816 | tf_op jit(solution)/shard_map/all_gather | solution.py:103
  68.0 11.8 %gather_fusion.3 = f32[2048]{0:T(1024)S(1)} fusion(f32[8192]{0:T(1024)S(1)} %bitcast.177, s32[2048]{0:T(1024)S(1)} %broadcast_clamp_fusion), kind=kCustom, calls=%fused_computation.9 | custom fusion | bytes 24576 | tf_op jit(solution)/shard_map/gather | solution.py:109
  79.8 11.8 %gather_fusion.2 = f32[2048]{0:T(1024)S(1)} fusion(f32[8192]{0:T(1024)S(1)} %bitcast.178, s32[2048]{0:T(1024)S(1)} %broadcast_clamp_fusion.1), kind=kCustom, calls=%fused_computation.8 | custom fusion | bytes 24576 | tf_op jit(solution)/shard_map/gather | solution.py:109
  108.2 18.6 %all-gather = f32[16,1,512]{2,1,0:T(1,128)S(1)} all-gather(f32[1,1,512]{2,1,0:T(1,128)S(1)} %convolution_bitcast_fusion.1), channel_id=1, replica_groups=mesh['grp'=2,'blk'=16] {'blk'}, dimensions={0}, use_global_device_ids=true | all-gather | bytes 34816 | tf_op jit(solution)/shard_map/all_gather | solution.py:102
  126.8 11.8 %gather_fusion.1 = f32[2048]{0:T(1024)S(1)} fusion(f32[8192]{0:T(1024)S(1)} %bitcast.175, s32[2048]{0:T(1024)S(1)} %broadcast_clamp_fusion), kind=kCustom, calls=%fused_computation.7 | custom fusion | bytes 24576 | tf_op jit(solution)/shard_map/gather | solution.py:108
  138.6 11.8 %gather_fusion = f32[2048]{0:T(1024)S(1)} fusion(f32[8192]{0:T(1024)S(1)} %bitcast.176, s32[2048]{0:T(1024)S(1)} %broadcast_clamp_fusion.1), kind=kCustom, calls=%fused_computation.6 | custom fusion | bytes 24576 | tf_op jit(solution)/shard_map/gather | solution.py:108
  151.0 11.3 %scatter_custom_fusion = f32[8192]{0:T(1024)S(1)} fusion(s32[2048]{0:T(1024)S(1)} %bitcast.200, f32[2048]{0:T(1024)S(1)} %get-tuple-element.110, f32[]{:T(128)} %constant.206.clone.1), kind=kCustom, calls=%fused_computation.137 | custom fusion | flops 2048 | bytes 32772 | tf_op jit(solution)/shard_map/scatter-add | solution.py:114
  162.3 11.6 %scatter_fusion = f32[8192]{0:T(1024)S(1)} fusion(f32[8192]{0:T(1024)S(1)} %scatter_custom_fusion, s32[2048]{0:T(1024)S(1)} %bitcast.198, f32[2048]{0:T(1024)S(1)} %get-tuple-element.109), kind=kCustom, calls=%fused_computation.11 | custom fusion | flops 2048 | bytes 32768 | tf_op jit(solution)/shard_map/scatter-add | solution.py:114
  173.9 58.2 %all-reduce = f32[8192]{0:T(1024)S(1)} all-reduce(f32[8192]{0:T(1024)S(1)} %scatter_fusion), channel_id=2, replica_groups=mesh['grp'=2,'blk'=16] {'blk'}, use_global_device_ids=true, to_apply=%region_7.9.clone | all-reduce | flops 8192 | bytes 65536
  243.2 3.4 fusion.102
  248.5 4.5 collective-permute-start.7
  263.3 3.2 multiply_bitcast_fusion.1
  272.2 4.1 collective-permute-start.9
  277.6 6.0 collective-permute-done.8
  303.9 35.1 %all-reduce.1 = (f32[1]{0:T(128)}, f32[128]{0:T(128)}) all-reduce(f32[1]{0:T(128)} %bitcast.25, f32[128]{0:T(128)S(1)} %convolution_bitcast_fusion.2), channel_id=1, replica_groups=mesh['grp'=2,'blk'=16] {'blk'}, use_global_device_ids=true, to_apply=%region_4.6 | all-reduce | flops 129 | bytes 1032 | tf_op jit(solution)/shard_map/psum | solution.py:158
  345.5 18.2 %reduce-scatter.24.cloned.1.call-done = f32[16,256]{1,0:T(8,128)} async-done(((f32[256,256]{1,0:T(8,128)}), f32[16,256]{1,0:T(8,128)}) %reduce-scatter.24.cloned.1.call-update) | async-done | bytes 16400
  364.6 57.0 %reduce-scatter.22.cloned.1.call-done = f32[16,256]{1,0:T(8,128)} async-done(((f32[256,256]{1,0:T(8,128)}), f32[16,256]{1,0:T(8,128)}) %reduce-scatter.22.cloned.1.call-update) | async-done | bytes 16400
  422.5 56.9 %reduce-scatter.18.cloned.1.call-done = f32[16,256]{1,0:T(8,128)} async-done(((f32[256,256]{1,0:T(8,128)}), f32[16,256]{1,0:T(8,128)}) %reduce-scatter.18.cloned.1.call-update) | async-done | bytes 16400 | tf_op jit(solution)/shard_map/reduce_scatter | solution.py:135
  479.4 57.7 %reduce-scatter.16.cloned.1.call-done = f32[16,256]{1,0:T(8,128)} async-done(((f32[256,256]{1,0:T(8,128)}), f32[16,256]{1,0:T(8,128)}) %reduce-scatter.16.cloned.1.call-update) | async-done | bytes 16400 | tf_op jit(solution)/shard_map/reduce_scatter | solution.py:135
  537.1 57.7 %reduce-scatter.14.cloned.1.call-done = f32[16,256]{1,0:T(8,128)} async-done(((f32[256,256]{1,0:T(8,128)}), f32[16,256]{1,0:T(8,128)}) %reduce-scatter.14.cloned.1.call-update) | async-done | bytes 16400 | tf_op jit(solution)/shard_map/reduce_scatter | solution.py:135
  596.8 56.2 %reduce-scatter.20.cloned.1.call-done = f32[16,128]{1,0:T(8,128)} async-done(((f32[256,128]{1,0:T(8,128)}), f32[16,128]{1,0:T(8,128)}) %reduce-scatter.20.cloned.1.call-update) | async-done | bytes 8208 | tf_op jit(solution)/shard_map/reduce_scatter | solution.py:121
  (219 shorter events, 104.1 us)
Async XLA Ops:
  7.2 333.2 %reduce-scatter.26.cloned.1.call-start = ((), (), s32[]{:S(2)}) async-start(), calls=%async_computation.13 | async-start | bytes 278528
  8.3 9.4 %collective-permute-start = (bf16[256,256]{1,0:T(8,128)(2,1)S(1)}, bf16[256,256]{1,0:T(8,128)(2,1)S(1)}, u32[]{:S(2)}, u32[]{:S(2)}) collective-permute-start(bf16[256,256]{1,0:T(8,128)(2,1)S(1)} %get-tuple-element.127), channel_id=1, source_target_pairs={{0,1},{1,2},{2,3},{3,4},{4,5},{5,6},{6,7},{7,8},{8,9},{9,10},{10,1... | collective-permute-start | bytes 393224 | tf_op jit(solution)/shard_map/ppermute | solution.py:20
  8.8 8.9 %collective-permute-start.1 = (bf16[256,256]{1,0:T(8,128)(2,1)S(1)}, bf16[256,256]{1,0:T(8,128)(2,1)S(1)}, u32[]{:S(2)}, u32[]{:S(2)}) collective-permute-start(bf16[256,256]{1,0:T(8,128)(2,1)S(1)} %get-tuple-element.128), channel_id=1, source_target_pairs={{1,0},{2,1},{3,2},{4,3},{5,4},{6,5},{7,6},{8,7},{9,8},{10,9},{11,1... | collective-permute-start | bytes 393224 | tf_op jit(solution)/shard_map/ppermute | solution.py:22
  16.5 220.5 %copy-start.27 = (pred[16]{0:T(512)(128)(4,1)}, pred[16]{0:T(512)(128)(4,1)S(1)}, u32[]{:S(2)}) copy-start(pred[16]{0:T(512)(128)(4,1)S(1)} %get-tuple-element.154) | copy-start | bytes 52
  28.9 7.1 %collective-permute-start.2 = (bf16[256,256]{0,1:T(8,128)(2,1)S(1)}, bf16[256,256]{0,1:T(8,128)(2,1)S(1)}, u32[]{:S(2)}, u32[]{:S(2)}) collective-permute-start(bf16[256,256]{0,1:T(8,128)(2,1)S(1)} %get-tuple-element.125), channel_id=1, source_target_pairs={{0,1},{1,2},{2,3},{3,4},{4,5},{5,6},{6,7},{7,8},{8,9},{9,10},{10,1... | collective-permute-start | bytes 393224 | tf_op jit(solution)/shard_map/ppermute | solution.py:20
  29.0 7.1 %collective-permute-start.3 = (bf16[256,256]{0,1:T(8,128)(2,1)S(1)}, bf16[256,256]{0,1:T(8,128)(2,1)S(1)}, u32[]{:S(2)}, u32[]{:S(2)}) collective-permute-start(bf16[256,256]{0,1:T(8,128)(2,1)S(1)} %get-tuple-element.126), channel_id=1, source_target_pairs={{1,0},{2,1},{3,2},{4,3},{5,4},{6,5},{7,6},{8,7},{9,8},{10,9},{11,1... | collective-permute-start | bytes 393224 | tf_op jit(solution)/shard_map/ppermute | solution.py:22
  45.5 47.9 %collective-permute-start.4 = (bf16[256,256]{0,1:T(8,128)(2,1)S(1)}, bf16[256,256]{0,1:T(8,128)(2,1)S(1)}, u32[]{:S(2)}, u32[]{:S(2)}) collective-permute-start(bf16[256,256]{0,1:T(8,128)(2,1)S(1)} %get-tuple-element.123), channel_id=1, source_target_pairs={{0,1},{1,2},{2,3},{3,4},{4,5},{5,6},{6,7},{7,8},{8,9},{9,10},{10,1... | collective-permute-start | bytes 393224 | tf_op jit(solution)/shard_map/ppermute | solution.py:20
  45.5 47.9 %collective-permute-start.5 = (bf16[256,256]{0,1:T(8,128)(2,1)S(1)}, bf16[256,256]{0,1:T(8,128)(2,1)S(1)}, u32[]{:S(2)}, u32[]{:S(2)}) collective-permute-start(bf16[256,256]{0,1:T(8,128)(2,1)S(1)} %get-tuple-element.124), channel_id=1, source_target_pairs={{1,0},{2,1},{3,2},{4,3},{5,4},{6,5},{7,6},{8,7},{9,8},{10,9},{11,1... | collective-permute-start | bytes 393224 | tf_op jit(solution)/shard_map/ppermute | solution.py:22
  107.3 126.5 %copy-start.25 = (f32[512]{0:T(512)}, f32[512]{0:T(512)S(1)}, u32[]{:S(2)}) copy-start(f32[512]{0:T(512)S(1)} %get-tuple-element.137) | copy-start | bytes 6148
  162.3 69.9 %copy-start.21 = (f32[512,128]{1,0:T(8,128)S(1)}, f32[512,128]{1,0:T(8,128)}, u32[]{:S(2)}) copy-start(f32[512,128]{1,0:T(8,128)} %copy-done.20) | copy-start | bytes 786436
  162.3 69.9 %copy-start.37 = (f32[128]{0:T(128)S(1)}, f32[128]{0:T(128)}, u32[]{:S(2)}) copy-start(f32[128]{0:T(128)} %param.35) | copy-start | bytes 1540
  247.5 7.3 %collective-permute-start.6 = (bf16[2,128,256]{2,0,1:T(2,128)(2,1)}, bf16[2,128,256]{2,0,1:T(2,128)(2,1)S(1)}, u32[]{:S(2)}, u32[]{:S(2)}) collective-permute-start(bf16[2,128,256]{2,0,1:T(2,128)(2,1)} %get-tuple-element.122), channel_id=1, source_target_pairs={{0,1},{1,2},{2,3},{3,4},{4,5},{5,6},{6,7},{7,8},{8,9},{9,10},{10,1... | collective-permute-start | bytes 393224 | tf_op jit(solution)/shard_map/ppermute | solution.py:31
  248.5 115.3 %reduce-scatter.24.cloned.1.call-start = ((), (), s32[]{:S(2)}) async-start(), calls=%async_computation.12 | async-start | bytes 278528
  248.5 7.7 %collective-permute-start.7 = (bf16[2,128,256]{2,0,1:T(2,128)(2,1)}, bf16[2,128,256]{2,0,1:T(2,128)(2,1)S(1)}, u32[]{:S(2)}, u32[]{:S(2)}) collective-permute-start(bf16[2,128,256]{2,0,1:T(2,128)(2,1)} %get-tuple-element.121), channel_id=1, source_target_pairs={{0,15},{1,0},{2,1},{3,2},{4,3},{5,4},{6,5},{7,6},{8,7},{9,8},{10,9... | collective-permute-start | bytes 393224 | tf_op jit(solution)/shard_map/ppermute | solution.py:31
  272.2 12.9 %collective-permute-start.9 = (bf16[2,128,256]{2,0,1:T(2,128)(2,1)S(1)}, bf16[2,128,256]{2,0,1:T(2,128)(2,1)S(1)}, u32[]{:S(2)}, u32[]{:S(2)}) collective-permute-start(bf16[2,128,256]{2,0,1:T(2,128)(2,1)S(1)} %get-tuple-element.119), channel_id=1, source_target_pairs={{0,15},{1,0},{2,1},{3,2},{4,3},{5,4},{6,5},{7,6},{8,7},{9,8},{10,9... | collective-permute-start | bytes 393224 | tf_op jit(solution)/shard_map/ppermute | solution.py:31
  276.2 7.4 %collective-permute-start.8 = (bf16[2,128,256]{2,0,1:T(2,128)(2,1)S(1)}, bf16[2,128,256]{2,0,1:T(2,128)(2,1)S(1)}, u32[]{:S(2)}, u32[]{:S(2)}) collective-permute-start(bf16[2,128,256]{2,0,1:T(2,128)(2,1)S(1)} %get-tuple-element.120), channel_id=1, source_target_pairs={{0,1},{1,2},{2,3},{3,4},{4,5},{5,6},{6,7},{7,8},{8,9},{9,10},{10,1... | collective-permute-start | bytes 393224 | tf_op jit(solution)/shard_map/ppermute | solution.py:31
  277.4 144.3 %reduce-scatter.22.cloned.1.call-start = ((), (), s32[]{:S(2)}) async-start(), calls=%async_computation.11 | async-start | bytes 278528
  290.5 188.9 %reduce-scatter.18.cloned.1.call-start = ((), (), s32[]{:S(2)}) async-start(), calls=%async_computation.9 | async-start | bytes 278528 | tf_op jit(solution)/shard_map/reduce_scatter | solution.py:135
  291.5 245.5 %reduce-scatter.16.cloned.1.call-start = ((), (), s32[]{:S(2)}) async-start(), calls=%async_computation.8 | async-start | bytes 278528 | tf_op jit(solution)/shard_map/reduce_scatter | solution.py:135
  292.6 302.2 %reduce-scatter.14.cloned.1.call-start = ((), (), s32[]{:S(2)}) async-start(), calls=%async_computation.7 | async-start | bytes 278528 | tf_op jit(solution)/shard_map/reduce_scatter | solution.py:135
  293.6 359.3 %reduce-scatter.20.cloned.1.call-start = ((), (), s32[]{:S(2)}) async-start(), calls=%async_computation.10 | async-start | bytes 139264 | tf_op jit(solution)/shard_map/reduce_scatter | solution.py:121
  303.5 37.8 %collective-permute-start.10 = (bf16[2,128,256]{2,0,1:T(2,128)(2,1)S(1)}, bf16[2,128,256]{2,0,1:T(2,128)(2,1)S(1)}, u32[]{:S(2)}, u32[]{:S(2)}) collective-permute-start(bf16[2,128,256]{2,0,1:T(2,128)(2,1)S(1)} %get-tuple-element.118), channel_id=1, source_target_pairs={{0,1},{1,2},{2,3},{3,4},{4,5},{5,6},{6,7},{7,8},{8,9},{9,10},{10,1... | collective-permute-start | bytes 393224 | tf_op jit(solution)/shard_map/ppermute | solution.py:31
  303.9 39.5 %copy-start.2 = (f32[512,256]{0,1:T(8,128)S(1)}, f32[512,256]{0,1:T(8,128)}, u32[]{:S(2)}) copy-start(f32[512,256]{0,1:T(8,128)} %copy-done.1) | copy-start | bytes 1572868
  339.0 3.8 collective-permute-start.11
  (35 other events, 232.8 us)
Sparse Core Ops, SparseCore 0:
  248.6 57.1 reduce-scatter.25
  309.4 54.3 reduce-scatter.23
  367.3 54.2 reduce-scatter.21
  425.0 54.3 reduce-scatter.17
  482.7 54.2 reduce-scatter.15
  540.4 54.3 reduce-scatter.13
  598.8 54.1 reduce-scatter.19
where the time goes:
time: 661 us; the launch traced here: 660 us
  waiting for transfers between devices  313 us (47%)
  blocking collectives  130 us (20%)
  local copies, waits for them, and re-layouts  86.1 us (13%)
  matrix products  53.3 us (8%)
  other arithmetic  36.9 us (6%)
  starting transfers between devices  23.8 us (4%)
  between operations  17.1 us (3%)
    reduce_scatter x3, waiting for transfers between devices, shards(): lax.psum_scatter(msg_term, 'blk', scatter_dimension=0, tiled=True)  172 us
    unnamed x10, waiting for transfers between devices  75.4 us
    unnamed x1, blocking collectives  58.2 us
    reduce_scatter x1, waiting for transfers between devices, shards(): lax.psum_scatter(dec_part, 'blk', scatter_dimension=0, tiled=True)  56.2 us
    psum x1, blocking collectives, shards(): lax.psum((objective_part.reshape(1), head_part), 'blk')  35.1 us
    gather x2, local copies, waits for them, and re-layouts, shards(): margin = all_scores[first] - all_scores[second]  23.6 us
    gather x2, local copies, waits for them, and re-layouts, shards(): wanted = jax.nn.sigmoid(all_targets[first] - all_targets[second])  23.6 us
    scatter-add x2, other arithmetic, shards(): jnp.zeros((node_total,), jnp.float32).at[first].add(d_margin).at[second]  22.8 us
  transfers between devices with their start and end apart: 19, of which 9 were waited for; matrix products, arithmetic and copies ran while one was open for 12% of the time, Pallas kernels for 0%

commit v1 on v0

v1 whole, which is shorter than its diff:
```python
import functools

import jax
import jax.numpy as jnp
from jax import lax
from jax.experimental import pallas as pl
from jax.experimental.pallas import tpu as pltpu
from jax.sharding import PartitionSpec as P

LAYERS = 3
HB = 2
TABLE_ROWS = 8
PAIR_CHUNK = 512
norm_eps = 1e-05

F32 = jnp.float32
BF16 = jnp.bfloat16


def dot_nn(a, b):
    return jnp.dot(a, b, preferred_element_type=F32)


def dot_nt(a, b):
    return lax.dot_general(a, b, (((1,), (1,)), ((), ())), preferred_element_type=F32)


def dot_tn(a, b):
    return lax.dot_general(a, b, (((0,), (0,)), ((), ())), preferred_element_type=F32)


def two_parts(values):
    upper = values.astype(BF16)
    return upper, (values - upper.astype(F32)).astype(BF16)


def step(
    n,
    tile_rows,
    tile_cols,
    tile_live,
    feat,
    vals,
    w_msg,
    w_self,
    w_dec,
    w_head,
    pairs,
    targets,
    grad_input,
    grad_msg,
    grad_self,
    grad_dec,
    small_out,
    band,
    rim,
    halo,
    hidden,
    message,
    update,
    slope,
    inverse,
    pooled,
    activ,
    head_slope,
    d_pooled,
    carried,
    d_update,
    d_mixed,
    d_message,
    d_halo,
    table,
    d_part,
    d_recv,
    small,
    small_recv,
    dec_part,
    dec_recv,
    w_part,
    w_recv,
    near_send,
    near_recv,
    all_send,
    all_recv,
):
    row_count, width = feat.shape
    slots, tile, _ = vals.shape
    per_device = row_count // tile
    half = HB * tile
    rows_out = width // n
    pair_total = pairs.shape[1]
    block_total = per_device * n
    me = lax.axis_index("blk")
    left, right = lax.rem(me + n - 1, n), lax.rem(me + 1, n)

    def each_peer(act):
        def visit(k, carry):
            act(lax.rem(me + k, n))
            return carry

        lax.fori_loop(1, n, visit, 0)

    barrier = pltpu.get_barrier_semaphore()
    each_peer(
        lambda peer: pl.semaphore_signal(
            barrier, inc=1, device_id={"blk": peer}, device_id_type=pl.DeviceIdType.MESH
        )
    )
    pl.semaphore_wait(barrier, n - 1)

    def near(source, target, kind, side):
        return pltpu.make_async_remote_copy(
            src_ref=source,
            dst_ref=target,
            send_sem=near_send.at[kind, side],
            recv_sem=near_recv.at[kind, 1 - side],
            device_id={"blk": (left, right)[side]},
            device_id_type=pl.DeviceIdType.MESH,
        )

    def near_arrival(target, kind, side):
        return pltpu.make_async_remote_copy(
            src_ref=target,
            dst_ref=target,
            send_sem=near_send.at[kind, side],
            recv_sem=near_recv.at[kind, side],
            device_id={"blk": left},
            device_id_type=pl.DeviceIdType.MESH,
        )

    def far(source, target, kind, peer, slot):
        return pltpu.make_async_remote_copy(
            src_ref=source,
            dst_ref=target,
            send_sem=all_send.at[kind, peer],
            recv_sem=all_recv.at[kind, slot],
            device_id={"blk": peer},
            device_id_type=pl.DeviceIdType.MESH,
        )

    def scatter(parts, received, kind):
        each_peer(lambda peer: far(parts.at[peer], received.at[me], kind, peer, me).start())

    def arrived(received, kind):
        each_peer(lambda peer: far(received.at[peer], received.at[peer], kind, peer, peer).wait_recv())

    def all_sent(part, kind):
        each_peer(lambda peer: far(part, part, kind, peer, me).wait_send())

    halves = (pl.ds(0, half), pl.ds(row_count - half, half))
    middle = pl.ds(half, row_count)
    rim_cols = (pl.ds(0, half), pl.ds(half + row_count, half))
    sent = []

    def send_halves(source, target, kind, side):
        copy = near(source.at[halves[side]], target.at[1 - side], kind, side)
        copy.start()
        sent.append(copy)

    for side in range(2):
        send_halves(feat, halo.at[0], 0, side)

    for r in range(per_device):
        for e in range(HB, per_device + HB):
            if not r <= e <= r + 2 * HB:
                band[pl.ds(r * tile, tile), pl.ds(e * tile, tile)] = jnp.zeros((tile, tile), BF16)
    for r in range(1, HB):
        for e in range(r):
            band[pl.ds(r * tile, tile), pl.ds(e * tile, tile)] = jnp.zeros((tile, tile), BF16)
            far_row, far_col = per_device - 1 - r, per_device + 2 * HB - 1 - e
            band[pl.ds(far_row * tile, tile), pl.ds(far_col * tile, tile)] = jnp.zeros((tile, tile), BF16)
    live = tile_live[0]

    def fill_row(r, carry):
        totals = [jnp.zeros((tile, tile), F32)] * (2 * HB + 1)
        for t in range(slots):
            shift = lax.rem(tile_cols[t] - tile_rows[t] + HB + block_total, block_total)
            here = jnp.logical_and(tile_rows[t] - me * per_device == r, t < live)
            values = vals[t].astype(F32)
            for d in range(2 * HB + 1):
                chosen = jnp.where(jnp.logical_and(here, shift == d), 1.0, 0.0).astype(F32)
                totals[d] = totals[d] + values * chosen
        at_row = pl.ds(pl.multiple_of(r * tile, tile), tile)
        for d in range(2 * HB + 1):
            at_col = pl.ds(pl.multiple_of((r + d) * tile, tile), tile)
            band[at_row, at_col] = totals[d].astype(BF16)
        return carry

    lax.fori_loop(0, per_device, fill_row, 0)
    for side in range(2):
        copy = near(band.at[halves[side], rim_cols[side]], rim.at[1 - side], 6, side)
        copy.start()
        sent.append(copy)

    for layer in range(LAYERS):
        source = feat if layer == 0 else hidden.at[layer - 1]
        centre = dot_nn(band[:, middle], source[...])
        for side in range(2):
            rows = halves[side]
            near_arrival(halo.at[layer, side], layer, side).wait_recv()
            term = dot_nn(band[rows, rim_cols[side]], halo[layer, side])
            here = centre[side * half : (side + 1) * half] + term
            msg = here.astype(BF16)
            message[layer, rows] = msg
            old = source[rows]
            mixed = dot_nn(msg, w_msg[layer]) + dot_nn(old, w_self[layer])
            squash = jax.nn.sigmoid(mixed)
            upd = old.astype(F32) + mixed * squash
            inv = lax.rsqrt(jnp.sum(upd * upd, axis=-1, keepdims=True) * (1.0 / width) + norm_eps)
            hidden[layer, rows] = (upd * inv).astype(BF16)
            if layer + 1 < LAYERS:
                send_halves(hidden.at[layer], halo.at[layer + 1], layer + 1, side)
            update[layer, rows] = upd
            inverse[layer, rows] = inv
            slope[layer, rows] = squash * (1.0 + mixed * (1.0 - squash))

    pool = hidden[0].astype(F32)
    for layer in range(1, LAYERS):
        pool = pool + hidden[layer].astype(F32)
    pooled[...] = pool.astype(BF16)
    pre_head = dot_nn(pooled[...], w_dec[...])
    squash = jax.nn.sigmoid(pre_head)
    act = pre_head * squash
    activ[...] = act
    head_slope[...] = squash * (1.0 + pre_head * (1.0 - squash))
    head_row = w_head[...]
    own_rows = []
    for b in range(per_device):
        block = act[b * tile : (b + 1) * tile] * head_row
        own_rows.append(jnp.sum(jnp.transpose(block), axis=0, keepdims=True))
    own_rows.append(targets[...])
    table[me] = jnp.concatenate(own_rows, axis=0)
    each_peer(lambda peer: far(table.at[me], table.at[me], 0, peer, me).start())
    arrived(table, 0)

    table_rows = n * TABLE_ROWS
    upper, lower = two_parts(table[...].reshape(table_rows, tile))
    chunk = min(PAIR_CHUNK, pair_total)
    total_d = jnp.zeros((table_rows, tile), F32)
    loss = jnp.zeros((1, chunk), F32)
    for c in range(pair_total // chunk):
        span = slice(c * chunk, (c + 1) * chunk)
        index = jnp.concatenate([pairs[0:1, span], pairs[1:2, span]], axis=1)
        lanes = lax.broadcasted_iota(jnp.int32, (tile, 2 * chunk), 0)
        low_hot = jnp.where(lanes == (index & (tile - 1)), 1.0, 0.0).astype(BF16)
        block_id = index >> 7
        place = lax.shift_right_logical(block_id, 2) * TABLE_ROWS + (block_id & 3)
        found = dot_nn(upper, low_hot) + dot_nn(lower, low_hot)
        at_row = lax.broadcasted_iota(jnp.int32, (table_rows, 2 * chunk), 0)
        in_scores = at_row == place
        score = jnp.sum(jnp.where(in_scores, found, 0.0), axis=0, keepdims=True)
        target = jnp.sum(jnp.where(at_row == place + 4, found, 0.0), axis=0, keepdims=True)
        margin = score[:, :chunk] - score[:, chunk:]
        wanted = jax.nn.sigmoid(target[:, :chunk] - target[:, chunk:])
        softplus = jnp.maximum(margin, 0.0) + jnp.log1p(jnp.exp(-jnp.abs(margin)))
        loss = loss + (softplus - wanted * margin)
        d_margin = (jax.nn.sigmoid(margin) - wanted) * (1.0 / pair_total)
        d_both = jnp.concatenate([d_margin, -d_margin], axis=1)
        d_upper = d_both.astype(BF16).astype(F32)
        d_lower = d_both - d_upper
        total_d = total_d + dot_nt(jnp.where(in_scores, d_upper, 0.0).astype(BF16), low_hot)
        total_d = total_d + dot_nt(jnp.where(in_scores, d_lower, 0.0).astype(BF16), low_hot)
    d_part[...] = total_d.reshape(n, TABLE_ROWS, tile)
    scatter(d_part, d_recv, 1)
    d_recv[me] = d_part[me]
    loss_here = jnp.sum(loss, axis=1, keepdims=True) * (1.0 / pair_total)
    arrived(d_recv, 1)
    d_scores = jnp.sum(d_recv[...], axis=0)

    head_sum = jnp.zeros((1, tile), F32)
    for b in range(per_device):
        rows = pl.ds(b * tile, tile)
        column = jnp.transpose(jnp.broadcast_to(d_scores[b : b + 1, :], (tile, tile)))
        head_sum = head_sum + jnp.sum(activ[rows] * column, axis=0, keepdims=True)
        d_pre = (column * head_row * head_slope[rows]).astype(BF16)
        d_mixed[rows, pl.ds(0, tile)] = d_pre
    d_pre = d_mixed[:, pl.ds(0, tile)]
    pooled_grad = dot_nt(d_pre, w_dec[...])
    d_pooled[...] = pooled_grad
    carried[...] = pooled_grad

    def weight_sends(layer):
        msg_term = dot_tn(message[layer], d_mixed[...])
        own = feat[...] if layer == 0 else hidden[layer - 1]
        self_term = dot_tn(own, d_mixed[...])
        for j in range(n):
            cut = slice(j * rows_out, (j + 1) * rows_out)
            w_part[layer, j, 0] = msg_term[cut].astype(w_part.dtype)
            w_part[layer, j, 1] = self_term[cut].astype(w_part.dtype)
        scatter(w_part.at[layer], w_recv.at[layer], 4 + layer)
        w_recv[layer, me] = w_part[layer, me]

    def weight_sums(layer):
        arrived(w_recv.at[layer], 4 + layer)
        total = jnp.sum(w_recv[layer].astype(F32), axis=0)
        grad_msg[layer] = total[0]
        grad_self[layer] = total[1]

    for layer in reversed(range(LAYERS)):
        if layer == LAYERS - 1:
            dec_term = dot_tn(pooled[...], d_pre)
        for side in range(2):
            rows = halves[side]
            inv = inverse[layer, rows]
            upd = update[layer, rows]
            carry = carried[rows]
            along = jnp.sum(carry * upd, axis=-1, keepdims=True) * (1.0 / width)
            d_upd = inv * carry - upd * (inv * inv * inv * along)
            d_update[rows] = d_upd
            mix = (d_upd * slope[layer, rows]).astype(BF16)
            d_mixed[rows] = mix
            d_message[layer, rows] = dot_nt(mix, w_msg[layer]).astype(BF16)
            send_halves(d_message.at[layer], d_halo.at[layer], 3 + layer, side)
        if layer == LAYERS - 1:
            for j in range(n):
                dec_part[j] = dec_term[j * rows_out : (j + 1) * rows_out].astype(dec_part.dtype)
            scatter(dec_part, dec_recv, 2)
            dec_recv[me] = dec_part[me]
            filler = jnp.zeros((TABLE_ROWS - 2, tile), F32)
            loss_row = jnp.broadcast_to(loss_here, (1, tile))
            small[...] = jnp.concatenate([head_sum, loss_row, filler], axis=0)
            each_peer(lambda peer: far(small, small_recv.at[me], 3, peer, me).start())
            small_recv[me] = small[...]
        weight_sends(layer)
        total = d_update[...] + dot_nt(d_mixed[...], w_self[layer])
        total = total + dot_tn(band[:, middle], d_message[layer])
        if layer > 0:
            total = total + d_pooled[...]
        else:
            arrived(dec_recv, 2)
            grad_dec[...] = jnp.sum(dec_recv[...].astype(F32), axis=0)
            arrived(small_recv, 3)
            small_out[...] = jnp.sum(small_recv[...], axis=0)
            weight_sums(2)
        result = carried if layer > 0 else grad_input
        for side in range(2):
            if layer == LAYERS - 1:
                near_arrival(rim.at[side], 6, side).wait_recv()
            near_arrival(d_halo.at[layer, side], 3 + layer, side).wait_recv()
            term = dot_tn(rim[side], d_halo[layer, side])
            result[halves[side]] = total[side * half : (side + 1) * half] + term
    weight_sums(1)
    weight_sums(0)
    for copy in sent:
        copy.wait_send()
    all_sent(table.at[me], 0)
    all_sent(d_part.at[me], 1)
    all_sent(dec_part.at[me], 2)
    all_sent(small, 3)
    for layer in range(LAYERS):
        all_sent(w_part.at[layer, me], 4 + layer)


def shards(
    features,
    tile_rows,
    tile_cols,
    tile_live,
    tile_vals,
    w_msg,
    w_self,
    w_dec,
    w_head,
    sample_pairs,
    targets,
):
    n = lax.axis_size("blk")
    row_count, width = features.shape
    tile = tile_vals.shape[1]
    per_device = row_count // tile
    dec = w_dec.shape[1]
    half = HB * tile
    rows_out = width // n
    wire = BF16 if rows_out % 16 == 0 else F32
    in_smem = pl.BlockSpec(memory_space=pltpu.SMEM)
    in_vmem = pl.BlockSpec(memory_space=pltpu.VMEM)
    outs = pl.pallas_call(
        functools.partial(step, n),
        out_shape=(
            jax.ShapeDtypeStruct((row_count, width), F32),
            jax.ShapeDtypeStruct((LAYERS, rows_out, width), F32),
            jax.ShapeDtypeStruct((LAYERS, rows_out, width), F32),
            jax.ShapeDtypeStruct((rows_out, dec), F32),
            jax.ShapeDtypeStruct((TABLE_ROWS, tile), F32),
        ),
        in_specs=[in_smem] * 3 + [in_vmem] * 8,
        out_specs=(in_vmem,) * 5,
        scratch_shapes=[
            pltpu.VMEM((row_count, row_count + 2 * half), BF16),
            pltpu.VMEM((2, half, half), BF16),
            pltpu.VMEM((LAYERS, 2, half, width), BF16),
            pltpu.VMEM((LAYERS, row_count, width), BF16),
            pltpu.VMEM((LAYERS, row_count, width), BF16),
            pltpu.VMEM((LAYERS, row_count, width), F32),
            pltpu.VMEM((LAYERS, row_count, width), F32),
            pltpu.VMEM((LAYERS, row_count, 1), F32),
            pltpu.VMEM((row_count, width), BF16),
            pltpu.VMEM((row_count, dec), F32),
            pltpu.VMEM((row_count, dec), F32),
            pltpu.VMEM((row_count, width), F32),
            pltpu.VMEM((row_count, width), F32),
            pltpu.VMEM((row_count, width), F32),
            pltpu.VMEM((row_count, width), BF16),
            pltpu.VMEM((LAYERS, row_count, width), BF16),
            pltpu.VMEM((LAYERS, 2, half, width), BF16),
            pltpu.VMEM((n, TABLE_ROWS, tile), F32),
            pltpu.VMEM((n, TABLE_ROWS, tile), F32),
            pltpu.VMEM((n, TABLE_ROWS, tile), F32),
            pltpu.VMEM((TABLE_ROWS, tile), F32),
            pltpu.VMEM((n, TABLE_ROWS, tile), F32),
            pltpu.VMEM((n, rows_out, dec), wire),
            pltpu.VMEM((n, rows_out, dec), wire),
            pltpu.VMEM((LAYERS, n, 2, rows_out, width), wire),
            pltpu.VMEM((LAYERS, n, 2, rows_out, width), wire),
            pltpu.SemaphoreType.DMA((7, 2)),
            pltpu.SemaphoreType.DMA((7, 2)),
            pltpu.SemaphoreType.DMA((7, n)),
            pltpu.SemaphoreType.DMA((7, n)),
        ],
        compiler_params=pltpu.CompilerParams(
            collective_id=0, has_side_effects=True, vmem_limit_bytes=56 * 1024 * 1024
        ),
        name="ranker_step",
    )(
        tile_rows,
        tile_cols,
        tile_live,
        features,
        tile_vals,
        w_msg,
        w_self,
        w_dec,
        w_head.reshape(1, dec),
        sample_pairs.T,
        targets.reshape(per_device, tile),
    )
    grad_input, grad_msg, grad_self, grad_dec, small = outs
    return small[1, :1], grad_msg, grad_self, grad_dec, small[0], grad_input


def solution(mesh):
    in_specs = (
        P(("grp", "blk"), None),
        P(("grp", "blk")),
        P(("grp", "blk")),
        P(("grp", "blk")),
        P(("grp", "blk"), None, None),
        P(),
        P(),
        P(),
        P(),
        P(("grp", "blk"), None),
        P(("grp", "blk")),
    )
    out_specs = (
        P("grp"),
        P("grp", "blk", None),
        P("grp", "blk", None),
        P(("grp", "blk"), None),
        P("grp"),
        P(("grp", "blk"), None),
    )
    return jax.shard_map(shards, mesh=mesh, in_specs=in_specs, out_specs=out_specs, check_vma=False)
```

time: 661 us -> 73.2 us (0.11)
  waiting for transfers between devices: 313 us -> 0 us
  blocking collectives: 130 us -> 0 us
  local copies, waits for them, and re-layouts: 86.1 us -> 6.95 us
  Pallas kernels: 0 us -> 64.6 us
  matrix products: 53.3 us -> 0 us
  other arithmetic: 36.9 us -> 0 us
  starting transfers between devices: 23.8 us -> 0 us
  between operations: 17.1 us -> 1.29 us
    reduce_scatter x4 -> x0, waiting for transfers between devices: 228 us -> none  [the longest x3 172 us: shards(): lax.psum_scatter(msg_term, 'blk', scatter_dimension=0, tiled=True)]
    unnamed x10 -> x0, waiting for transfers between devices: 75.4 us -> none
    pallas_call x0 -> x1, Pallas kernels: none -> 64.6 us  [shards(): pl.pallas_call(functools.partial(step, n), out_shape=(jax.ShapeDtypeStruc...]
    unnamed x1 -> x0, blocking collectives: 58.2 us -> none
    gather x10 -> x0, local copies, waits for them, and re-layouts: 54.2 us -> none  [the longest x2 23.6 us: shards(): margin = all_scores[first] - all_scores[second]]
    dot_general x33 -> x0, matrix products: 51.3 us -> none  [the longest x6 15.3 us: tile_products(): jnp.einsum(form, tile_vals, picked, preferred_element_type=jnp.float32)]
    all_gather x2 -> x0, blocking collectives: 36.5 us -> none  [the longest x1 18.6 us: shards(): lax.all_gather(scores, 'blk', axis=0, tiled=True)]
    psum x1 -> x0, blocking collectives: 35.1 us -> none  [shards(): lax.psum((objective_part.reshape(1), head_part), 'blk')]
  transfers between devices with their start and end apart: 19 -> 0, of which waited for: 9 -> 0; matrix products, arithmetic and copies ran while one was open for 12% -> 0% of each run, Pallas kernels for 0% -> 0%
where the time goes in v1:
time: 73.2 us; the launch traced here: 72.9 us
  Pallas kernels  64.6 us (88%)
  local copies, waits for them, and re-layouts  6.95 us (9%)
  between operations  1.29 us (2%)
    pallas_call x1, Pallas kernels, shards(): pl.pallas_call(functools.partial(step, n), out_shape=(jax.ShapeDtypeStruc...  64.6 us
    unnamed x8, local copies, waits for them, and re-layouts  4.59 us

profile of v1, /device:TPU:0, one launch (start us, length us, event | category | flops | bytes accessed | tf_op | source)
XLA Modules:
  0.0 72.9 jit_solution(1593454714939194325)
XLA Ops:
  1.3 64.6 %ranker_step.1 = (f32[512,256]{1,0:T(8,128)}, f32[3,16,256]{2,1,0:T(8,128)}, f32[3,16,256]{2,1,0:T(8,128)}, f32[16,128]{1,0:T(8,128)}, f32[8,128]{1,0:T(8,128)}) custom-call(s32[16]{0:T(128)} %tile_rows.1, s32[16]{0:T(128)} %tile_cols.1, s32[1]{0:T(128)S(6)} %copy.21.tile_live, bf16[512,256]{1,0:T(8,128)(2,1)} %feat.1, bf16[16,128,128]{2,1,0:T(8,128)(2,1)} %vals.1, ...), custom_call_target="tpu_custom_call" | custom-call | tf_op jit(solution)/shard_map/ranker_step/pallas_call | solution.py:377
  65.9 1.2 %slice.6 = f32[1,1]{1,0:T(1,128)} slice(f32[8,128]{1,0:T(8,128)} %get-tuple-element.11), slice={[1:2], [0:1]} | slice | bytes 8 | tf_op jit(solution)/shard_map/slice | solution.py:438
  67.1 1.2 %slice_bitcast_fusion = f32[128]{0:T(128)} fusion(f32[8,128]{1,0:T(8,128)} %get-tuple-element.11), kind=kLoop, calls=%fused_computation | loop fusion | bytes 1024 | tf_op jit(solution)/shard_map/squeeze | solution.py:438
  68.3 0.0 copy-start
  68.3 1.4 %copy.22 = f32[3,16,256]{2,1,0:T(8,128)} copy(f32[3,16,256]{2,1,0:T(8,128)} %get-tuple-element.23) | data formatting | bytes 98304
  69.7 0.0 copy-done
  69.7 0.0 copy-start.1
  69.7 0.6 copy.23
  70.3 0.1 copy-done.1
  70.4 0.6 copy.24
  71.0 1.9 %copy.25 = f32[512,256]{1,0:T(8,128)} copy(f32[512,256]{1,0:T(8,128)} %get-tuple-element.27) | data formatting | bytes 1048576
Async XLA Ops:
  68.3 1.4 %copy-start = (f32[3,16,256]{2,1,0:T(8,128)S(1)}, f32[3,16,256]{2,1,0:T(8,128)}, u32[]{:S(2)}) copy-start(f32[3,16,256]{2,1,0:T(8,128)} %get-tuple-element.24) | copy-start | bytes 147460
  69.7 0.7 copy-start.1

commit v2 on v1

--- a/solution.py
+++ b/solution.py
@@ -40,10 +40,10 @@
     tile_cols,
     tile_live,
     feat,
-    vals,
-    w_msg,
-    w_self,
-    w_dec,
+    vals_in,
+    w_msg_in,
+    w_self_in,
+    w_dec_in,
     w_head,
     pairs,
     targets,
@@ -52,6 +52,10 @@
     grad_self,
     grad_dec,
     small_out,
+    vals,
+    w_msg,
+    w_self,
+    w_dec,
     band,
     rim,
     halo,
@@ -77,7 +81,15 @@
     dec_part,
     dec_recv,
     w_part,
+    w_near,
+    w_sum,
     w_recv,
+    target_table,
+    load_sem,
+    pair_send,
+    pair_recv,
+    chip_send,
+    chip_recv,
     near_send,
     near_recv,
     all_send,
@@ -100,6 +112,16 @@
 
         lax.fori_loop(1, n, visit, 0)
 
+    loads = [
+        pltpu.make_async_copy(there, here, load_sem.at[i])
+        for i, (there, here) in enumerate(
+            ((vals_in, vals), (w_msg_in, w_msg), (w_self_in, w_self), (w_dec_in, w_dec))
+        )
+    ]
+    for load in loads:
+        load.start()
+    filler = jnp.zeros((TABLE_ROWS - per_device, tile), F32)
+    target_table[me] = jnp.concatenate([targets[...], filler], axis=0)
     barrier = pltpu.get_barrier_semaphore()
     each_peer(
         lambda peer: pl.semaphore_signal(
@@ -159,6 +181,9 @@
 
     for side in range(2):
         send_halves(feat, halo.at[0], 0, side)
+
+    each_peer(lambda peer: far(target_table.at[me], target_table.at[me], 4, peer, me).start())
+    loads[0].wait()
 
     for r in range(per_device):
         for e in range(HB, per_device + HB):
@@ -192,6 +217,8 @@
         copy.start()
         sent.append(copy)
 
+    for load in loads[1:]:
+        load.wait()
     for layer in range(LAYERS):
         source = feat if layer == 0 else hidden.at[layer - 1]
         centre = dot_nn(band[:, middle], source[...])
@@ -228,30 +255,37 @@
     for b in range(per_device):
         block = act[b * tile : (b + 1) * tile] * head_row
         own_rows.append(jnp.sum(jnp.transpose(block), axis=0, keepdims=True))
-    own_rows.append(targets[...])
+    own_rows.append(filler)
     table[me] = jnp.concatenate(own_rows, axis=0)
     each_peer(lambda peer: far(table.at[me], table.at[me], 0, peer, me).start())
-    arrived(table, 0)
-
+
+    arrived(target_table, 4)
     table_rows = n * TABLE_ROWS
-    upper, lower = two_parts(table[...].reshape(table_rows, tile))
     chunk = min(PAIR_CHUNK, pair_total)
-    total_d = jnp.zeros((table_rows, tile), F32)
-    loss = jnp.zeros((1, chunk), F32)
+    upper, lower = two_parts(target_table[...].reshape(table_rows, tile))
+    lanes = lax.broadcasted_iota(jnp.int32, (tile, 2 * chunk), 0)
+    at_row = lax.broadcasted_iota(jnp.int32, (table_rows, 2 * chunk), 0)
+    prepared = []
     for c in range(pair_total // chunk):
         span = slice(c * chunk, (c + 1) * chunk)
         index = jnp.concatenate([pairs[0:1, span], pairs[1:2, span]], axis=1)
-        lanes = lax.broadcasted_iota(jnp.int32, (tile, 2 * chunk), 0)
         low_hot = jnp.where(lanes == (index & (tile - 1)), 1.0, 0.0).astype(BF16)
         block_id = index >> 7
         place = lax.shift_right_logical(block_id, 2) * TABLE_ROWS + (block_id & 3)
         found = dot_nn(upper, low_hot) + dot_nn(lower, low_hot)
-        at_row = lax.broadcasted_iota(jnp.int32, (table_rows, 2 * chunk), 0)
+        target = jnp.sum(jnp.where(at_row == place, found, 0.0), axis=0, keepdims=True)
+        wanted = jax.nn.sigmoid(target[:, :chunk] - target[:, chunk:])
+        prepared.append((low_hot, place, wanted))
+    arrived(table, 0)
+
+    upper, lower = two_parts(table[...].reshape(table_rows, tile))
+    total_d = jnp.zeros((table_rows, tile), F32)
+    loss = jnp.zeros((1, chunk), F32)
+    for low_hot, place, wanted in prepared:
+        found = dot_nn(upper, low_hot) + dot_nn(lower, low_hot)
         in_scores = at_row == place
         score = jnp.sum(jnp.where(in_scores, found, 0.0), axis=0, keepdims=True)
-        target = jnp.sum(jnp.where(at_row == place + 4, found, 0.0), axis=0, keepdims=True)
         margin = score[:, :chunk] - score[:, chunk:]
-        wanted = jax.nn.sigmoid(target[:, :chunk] - target[:, chunk:])
         softplus = jnp.maximum(margin, 0.0) + jnp.log1p(jnp.exp(-jnp.abs(margin)))
         loss = loss + (softplus - wanted * margin)
         d_margin = (jax.nn.sigmoid(margin) - wanted) * (1.0 / pair_total)
@@ -285,13 +319,48 @@
         self_term = dot_tn(own, d_mixed[...])
         for j in range(n):
             cut = slice(j * rows_out, (j + 1) * rows_out)
-            w_part[layer, j, 0] = msg_term[cut].astype(w_part.dtype)
-            w_part[layer, j, 1] = self_term[cut].astype(w_part.dtype)
-        scatter(w_part.at[layer], w_recv.at[layer], 4 + layer)
-        w_recv[layer, me] = w_part[layer, me]
+            w_part[layer, j % 2, j // 2, 0] = msg_term[cut].astype(w_part.dtype)
+            w_part[layer, j % 2, j // 2, 1] = self_term[cut].astype(w_part.dtype)
+        beside(layer).start()
+
+    core, chip, chips = lax.rem(me, 2), me // 2, n // 2
+
+    def beside(layer):
+        return pltpu.make_async_remote_copy(
+            src_ref=w_part.at[layer, 1 - core],
+            dst_ref=w_near.at[layer],
+            send_sem=pair_send.at[layer],
+            recv_sem=pair_recv.at[layer],
+            device_id={"blk": me + 1 - 2 * core},
+            device_id_type=pl.DeviceIdType.MESH,
+        )
+
+    def chip_copy(layer, other, slot):
+        return pltpu.make_async_remote_copy(
+            src_ref=w_sum.at[layer, other],
+            dst_ref=w_recv.at[layer, slot],
+            send_sem=chip_send.at[layer, other],
+            recv_sem=chip_recv.at[layer, slot],
+            device_id={"blk": other * 2 + core},
+            device_id_type=pl.DeviceIdType.MESH,
+        )
+
+    def each_chip(act):
+        def visit(k, carry):
+            act(lax.rem(chip + k, chips))
+            return carry
+
+        lax.fori_loop(1, chips, visit, 0)
+
+    def chip_sends(layer):
+        beside(layer).wait_recv()
+        both = w_part[layer, core].astype(F32) + w_near[layer].astype(F32)
+        w_sum[layer] = both.astype(w_sum.dtype)
+        each_chip(lambda other: chip_copy(layer, other, chip).start())
+        w_recv[layer, chip] = w_sum[layer, chip]
 
     def weight_sums(layer):
-        arrived(w_recv.at[layer], 4 + layer)
+        each_chip(lambda other: chip_copy(layer, other, other).wait_recv())
         total = jnp.sum(w_recv[layer].astype(F32), axis=0)
         grad_msg[layer] = total[0]
         grad_self[layer] = total[1]
@@ -316,14 +385,15 @@
                 dec_part[j] = dec_term[j * rows_out : (j + 1) * rows_out].astype(dec_part.dtype)
             scatter(dec_part, dec_recv, 2)
             dec_recv[me] = dec_part[me]
-            filler = jnp.zeros((TABLE_ROWS - 2, tile), F32)
+            below = jnp.zeros((TABLE_ROWS - 2, tile), F32)
             loss_row = jnp.broadcast_to(loss_here, (1, tile))
-            small[...] = jnp.concatenate([head_sum, loss_row, filler], axis=0)
+            small[...] = jnp.concatenate([head_sum, loss_row, below], axis=0)
             each_peer(lambda peer: far(small, small_recv.at[me], 3, peer, me).start())
             small_recv[me] = small[...]
         weight_sends(layer)
         total = d_update[...] + dot_nt(d_mixed[...], w_self[layer])
         total = total + dot_tn(band[:, middle], d_message[layer])
+        chip_sends(layer)
         if layer > 0:
             total = total + d_pooled[...]
         else:
@@ -347,8 +417,18 @@
     all_sent(d_part.at[me], 1)
     all_sent(dec_part.at[me], 2)
     all_sent(small, 3)
+    all_sent(target_table.at[me], 4)
     for layer in range(LAYERS):
-        all_sent(w_part.at[layer, me], 4 + layer)
+        beside(layer).wait_send()
+        each_chip(lambda other: chip_copy(layer, other, chip).wait_send())
+
+
+def hand_out(*refs):
+    for source, target in zip(refs[:4], refs[5:9]):
+        target[...] = source[...]
+    small, grad_head, objective = refs[4], refs[9], refs[10]
+    grad_head[...] = small[0:1]
+    objective[...] = small[1:2, 0:1]
 
 
 def shards(
@@ -383,9 +463,13 @@
             jax.ShapeDtypeStruct((rows_out, dec), F32),
             jax.ShapeDtypeStruct((TABLE_ROWS, tile), F32),
         ),
-        in_specs=[in_smem] * 3 + [in_vmem] * 8,
+        in_specs=[in_smem] * 3 + [in_vmem] + [pl.BlockSpec(memory_space=pl.ANY)] * 4 + [in_vmem] * 3,
         out_specs=(in_vmem,) * 5,
         scratch_shapes=[
+            pltpu.VMEM(tile_vals.shape, BF16),
+            pltpu.VMEM(w_msg.shape, BF16),
+            pltpu.VMEM(w_self.shape, BF16),
+            pltpu.VMEM(w_dec.shape, BF16),
             pltpu.VMEM((row_count, row_count + 2 * half), BF16),
             pltpu.VMEM((2, half, half), BF16),
             pltpu.VMEM((LAYERS, 2, half, width), BF16),
@@ -410,12 +494,20 @@
             pltpu.VMEM((n, TABLE_ROWS, tile), F32),
             pltpu.VMEM((n, rows_out, dec), wire),
             pltpu.VMEM((n, rows_out, dec), wire),
-            pltpu.VMEM((LAYERS, n, 2, rows_out, width), wire),
-            pltpu.VMEM((LAYERS, n, 2, rows_out, width), wire),
+            pltpu.VMEM((LAYERS, 2, n // 2, 2, rows_out, width), wire),
+            pltpu.VMEM((LAYERS, n // 2, 2, rows_out, width), wire),
+            pltpu.VMEM((LAYERS, n // 2, 2, rows_out, width), wire),
+            pltpu.VMEM((LAYERS, n // 2, 2, rows_out, width), wire),
+            pltpu.VMEM((n, TABLE_ROWS, tile), F32),
+            pltpu.SemaphoreType.DMA((4,)),
+            pltpu.SemaphoreType.DMA((LAYERS,)),
+            pltpu.SemaphoreType.DMA((LAYERS,)),
+            pltpu.SemaphoreType.DMA((LAYERS, n // 2)),
+            pltpu.SemaphoreType.DMA((LAYERS, n // 2)),
             pltpu.SemaphoreType.DMA((7, 2)),
             pltpu.SemaphoreType.DMA((7, 2)),
-            pltpu.SemaphoreType.DMA((7, n)),
-            pltpu.SemaphoreType.DMA((7, n)),
+            pltpu.SemaphoreType.DMA((5, n)),
+            pltpu.SemaphoreType.DMA((5, n)),
         ],
         compiler_params=pltpu.CompilerParams(
             collective_id=0, has_side_effects=True, vmem_limit_bytes=56 * 1024 * 1024
@@ -434,8 +526,16 @@
         sample_pairs.T,
         targets.reshape(per_device, tile),
     )
-    grad_input, grad_msg, grad_self, grad_dec, small = outs
-    return small[1, :1], grad_msg, grad_self, grad_dec, small[0], grad_input
+    big = [jax.ShapeDtypeStruct(out.shape, F32) for out in outs[:4]]
+    grad_input, grad_msg, grad_self, grad_dec, grad_head, objective = pl.pallas_call(
+        hand_out,
+        out_shape=(*big, jax.ShapeDtypeStruct((1, dec), F32), jax.ShapeDtypeStruct((1, 1), F32)),
+        in_specs=[in_vmem] * 5,
+        out_specs=(in_vmem,) * 6,
+        compiler_params=pltpu.CompilerParams(vmem_limit_bytes=16 * 1024 * 1024),
+        name="hand_out",
+    )(*outs)
+    return objective.reshape(1), grad_msg, grad_self, grad_dec, grad_head.reshape(dec), grad_input
 
 
 def solution(mesh):

time: 73.2 us -> 64.5 us (0.88)
  Pallas kernels: 64.6 us -> 58.8 us
  local copies, waits for them, and re-layouts: 6.95 us -> 3.99 us
    pallas_call x1, Pallas kernels: 64.6 us -> 58 us  [shards(): pl.pallas_call(functools.partial(step, n), out_shape=(jax.ShapeDtypeStruc...]
    slice x1 -> x0, local copies, waits for them, and re-layouts: 1.18 us -> none  [shards(): return (small[1, :1], grad_msg, grad_self, grad_dec, small[0], grad_input)]
    squeeze x1 -> x0, local copies, waits for them, and re-layouts: 1.18 us -> none  [shards(): return (small[1, :1], grad_msg, grad_self, grad_dec, small[0], grad_input)]
    pallas_call x0 -> x1, Pallas kernels: none -> 0.86 us  [shards(): pl.pallas_call(hand_out, out_shape=(*big, jax.ShapeDtypeStruct((1, dec),...]
    unnamed x8 -> x10, local copies, waits for them, and re-layouts: 4.59 us -> 3.99 us
where the time goes in v2:
time: 64.5 us; the launch traced here: 64.1 us
  Pallas kernels  58.8 us (91%)
  local copies, waits for them, and re-layouts  3.99 us (6%)
  between operations  1.3 us (2%)
    pallas_call x1, Pallas kernels, shards(): pl.pallas_call(functools.partial(step, n), out_shape=(jax.ShapeDtypeStruc...  58 us
    unnamed x10, local copies, waits for them, and re-layouts  3.99 us

profile of v2, /device:TPU:0, one launch (start us, length us, event | category | flops | bytes accessed | tf_op | source)
XLA Modules:
  0.0 64.1 jit_solution(15268274053102735631)
XLA Ops:
  1.3 58.0 %ranker_step.1 = (f32[512,256]{1,0:T(8,128)}, f32[3,16,256]{2,1,0:T(8,128)}, f32[3,16,256]{2,1,0:T(8,128)}, f32[16,128]{1,0:T(8,128)}, f32[8,128]{1,0:T(8,128)}) custom-call(s32[16]{0:T(128)} %tile_rows.1, s32[16]{0:T(128)} %tile_cols.1, s32[1]{0:T(128)S(6)} %copy.17.tile_live, bf16[512,256]{1,0:T(8,128)(2,1)} %feat.1, bf16[16,128,128]{2,1,0:T(8,128)(2,1)} %vals_in.1, ...), custom_call_target="tpu_custom_call" | custom-call | tf_op jit(solution)/shard_map/ranker_step/pallas_call | solution.py:457
  59.2 0.0 copy-start.3
  59.3 0.7 %copy-done.3 = f32[16,128]{1,0:T(8,128)S(1)} copy-done((f32[16,128]{1,0:T(8,128)S(1)}, f32[16,128]{1,0:T(8,128)}, u32[]{:S(2)}) %copy-start.3) | copy-done | bytes 8216
  59.9 0.0 copy-start
  59.9 1.0 %copy-done = f32[512,256]{1,0:T(8,128)S(1)} copy-done((f32[512,256]{1,0:T(8,128)S(1)}, f32[512,256]{1,0:T(8,128)}, u32[]{:S(2)}) %copy-start) | copy-done | bytes 524312
  61.0 0.0 copy-start.1
  61.0 0.8 %copy-done.1 = f32[3,16,256]{2,1,0:T(8,128)S(1)} copy-done((f32[3,16,256]{2,1,0:T(8,128)S(1)}, f32[3,16,256]{2,1,0:T(8,128)}, u32[]{:S(2)}) %copy-start.1) | copy-done | bytes 49176
  61.8 0.0 copy-start.2
  61.8 0.8 %copy-done.2 = f32[3,16,256]{2,1,0:T(8,128)S(1)} copy-done((f32[3,16,256]{2,1,0:T(8,128)S(1)}, f32[3,16,256]{2,1,0:T(8,128)}, u32[]{:S(2)}) %copy-start.2) | copy-done | bytes 49176
  62.6 0.0 copy-start.4
  62.6 0.7 %copy-done.4 = f32[8,128]{1,0:T(8,128)S(1)} copy-done((f32[8,128]{1,0:T(8,128)S(1)}, f32[8,128]{1,0:T(8,128)}, u32[]{:S(2)}) %copy-start.4) | copy-done | bytes 4120
  63.3 0.9 %hand_out.1 = (f32[512,256]{1,0:T(8,128)}, f32[3,16,256]{2,1,0:T(8,128)}, f32[3,16,256]{2,1,0:T(8,128)}, f32[16,128]{1,0:T(8,128)}, f32[1,128]{1,0:T(1,128)}, /*index=5*/f32[1,1]{1,0:T(1,128)}) custom-call(f32[512,256]{1,0:T(8,128)S(1)} %copy-done, f32[3,16,256]{2,1,0:T(8,128)S(1)} %copy-done.1, f32[3,16,256]{2,1,0:T(8,128)S(1)} %copy-done.2, ...), custom_call_target="tpu_custom_call" | custom-call | tf_op jit(solution)/shard_map/hand_out/pallas_call | solution.py:530
Async XLA Ops:
  59.2 0.7 %copy-start.3 = (f32[16,128]{1,0:T(8,128)S(1)}, f32[16,128]{1,0:T(8,128)}, u32[]{:S(2)}) copy-start(f32[16,128]{1,0:T(8,128)} %get-tuple-element.20.refs_3_) | copy-start | bytes 24580
  59.9 1.0 %copy-start = (f32[512,256]{1,0:T(8,128)S(1)}, f32[512,256]{1,0:T(8,128)}, u32[]{:S(2)}) copy-start(f32[512,256]{1,0:T(8,128)} %get-tuple-element.17.refs_0_) | copy-start | bytes 1572868
  61.0 0.8 %copy-start.1 = (f32[3,16,256]{2,1,0:T(8,128)S(1)}, f32[3,16,256]{2,1,0:T(8,128)}, u32[]{:S(2)}) copy-start(f32[3,16,256]{2,1,0:T(8,128)} %get-tuple-element.18.refs_1_) | copy-start | bytes 147460
  61.8 0.8 %copy-start.2 = (f32[3,16,256]{2,1,0:T(8,128)S(1)}, f32[3,16,256]{2,1,0:T(8,128)}, u32[]{:S(2)}) copy-start(f32[3,16,256]{2,1,0:T(8,128)} %get-tuple-element.19.refs_2_) | copy-start | bytes 147460
  62.6 0.7 %copy-start.4 = (f32[8,128]{1,0:T(8,128)S(1)}, f32[8,128]{1,0:T(8,128)}, u32[]{:S(2)}) copy-start(f32[8,128]{1,0:T(8,128)} %get-tuple-element.21.refs_4_) | copy-start | bytes 12292

commit v3 on v2

--- a/solution.py
+++ b/solution.py
@@ -103,7 +103,8 @@
     pair_total = pairs.shape[1]
     block_total = per_device * n
     me = lax.axis_index("blk")
-    left, right = lax.rem(me + n - 1, n), lax.rem(me + 1, n)
+    core, chip, chips = lax.rem(me, 2), me // 2, n // 2
+    order = (1 - core, core)
 
     def each_peer(act):
         def visit(k, carry):
@@ -136,7 +137,7 @@
             dst_ref=target,
             send_sem=near_send.at[kind, side],
             recv_sem=near_recv.at[kind, 1 - side],
-            device_id={"blk": (left, right)[side]},
+            device_id={"blk": lax.rem(me + n - 1 + 2 * side, n)},
             device_id_type=pl.DeviceIdType.MESH,
         )
 
@@ -146,7 +147,7 @@
             dst_ref=target,
             send_sem=near_send.at[kind, side],
             recv_sem=near_recv.at[kind, side],
-            device_id={"blk": left},
+            device_id={"blk": lax.rem(me + n - 1, n)},
             device_id_type=pl.DeviceIdType.MESH,
         )
 
@@ -169,17 +170,22 @@
     def all_sent(part, kind):
         each_peer(lambda peer: far(part, part, kind, peer, me).wait_send())
 
-    halves = (pl.ds(0, half), pl.ds(row_count - half, half))
     middle = pl.ds(half, row_count)
-    rim_cols = (pl.ds(0, half), pl.ds(half + row_count, half))
+
+    def half_rows(side):
+        return pl.ds(pl.multiple_of(side * (row_count - half), tile), half)
+
+    def rim_cols(side):
+        return pl.ds(pl.multiple_of(side * (row_count + half), tile), half)
+
     sent = []
 
     def send_halves(source, target, kind, side):
-        copy = near(source.at[halves[side]], target.at[1 - side], kind, side)
+        copy = near(source.at[half_rows(side)], target.at[1 - side], kind, side)
         copy.start()
         sent.append(copy)
 
-    for side in range(2):
+    for side in order[::-1]:
         send_halves(feat, halo.at[0], 0, side)
 
     each_peer(lambda peer: far(target_table.at[me], target_table.at[me], 4, peer, me).start())
@@ -212,8 +218,8 @@
         return carry
 
     lax.fori_loop(0, per_device, fill_row, 0)
-    for side in range(2):
-        copy = near(band.at[halves[side], rim_cols[side]], rim.at[1 - side], 6, side)
+    for side in order[::-1]:
+        copy = near(band.at[half_rows(side), rim_cols(side)], rim.at[1 - side], 6, side)
         copy.start()
         sent.append(copy)
 
@@ -221,13 +227,12 @@
         load.wait()
     for layer in range(LAYERS):
         source = feat if layer == 0 else hidden.at[layer - 1]
-        centre = dot_nn(band[:, middle], source[...])
-        for side in range(2):
-            rows = halves[side]
+        carried[...] = dot_nn(band[:, middle], source[...])
+        for side in order:
+            rows = half_rows(side)
             near_arrival(halo.at[layer, side], layer, side).wait_recv()
-            term = dot_nn(band[rows, rim_cols[side]], halo[layer, side])
-            here = centre[side * half : (side + 1) * half] + term
-            msg = here.astype(BF16)
+            term = dot_nn(band[rows, rim_cols(side)], halo[layer, side])
+            msg = (carried[rows] + term).astype(BF16)
             message[layer, rows] = msg
             old = source[rows]
             mixed = dot_nn(msg, w_msg[layer]) + dot_nn(old, w_self[layer])
@@ -323,8 +328,6 @@
             w_part[layer, j % 2, j // 2, 1] = self_term[cut].astype(w_part.dtype)
         beside(layer).start()
 
-    core, chip, chips = lax.rem(me, 2), me // 2, n // 2
-
     def beside(layer):
         return pltpu.make_async_remote_copy(
             src_ref=w_part.at[layer, 1 - core],
@@ -368,8 +371,8 @@
     for layer in reversed(range(LAYERS)):
         if layer == LAYERS - 1:
             dec_term = dot_tn(pooled[...], d_pre)
-        for side in range(2):
-            rows = halves[side]
+        for side in order[::-1]:
+            rows = half_rows(side)
             inv = inverse[layer, rows]
             upd = update[layer, rows]
             carry = carried[rows]
@@ -402,13 +405,15 @@
             arrived(small_recv, 3)
             small_out[...] = jnp.sum(small_recv[...], axis=0)
             weight_sums(2)
+        d_update[...] = total
         result = carried if layer > 0 else grad_input
-        for side in range(2):
+        for side in order:
+            rows = half_rows(side)
             if layer == LAYERS - 1:
                 near_arrival(rim.at[side], 6, side).wait_recv()
             near_arrival(d_halo.at[layer, side], 3 + layer, side).wait_recv()
             term = dot_tn(rim[side], d_halo[layer, side])
-            result[halves[side]] = total[side * half : (side + 1) * half] + term
+            result[rows] = d_update[rows] + term
     weight_sums(1)
     weight_sums(0)
     for copy in sent:
@@ -424,11 +429,17 @@
 
 
 def hand_out(*refs):
-    for source, target in zip(refs[:4], refs[5:9]):
-        target[...] = source[...]
-    small, grad_head, objective = refs[4], refs[9], refs[10]
-    grad_head[...] = small[0:1]
-    objective[...] = small[1:2, 0:1]
+    sources, targets, (small, sems) = refs[:5], refs[5:11], refs[11:]
+    copies = [
+        pltpu.make_async_copy(source, target, sems.at[i])
+        for i, (source, target) in enumerate(zip(sources, (*targets[:4], small)))
+    ]
+    for copy in copies:
+        copy.start()
+    for copy in copies:
+        copy.wait()
+    targets[4][...] = small[0:1]
+    targets[5][...] = small[1:2, 0:1]
 
 
 def shards(
@@ -530,9 +541,13 @@
     grad_input, grad_msg, grad_self, grad_dec, grad_head, objective = pl.pallas_call(
         hand_out,
         out_shape=(*big, jax.ShapeDtypeStruct((1, dec), F32), jax.ShapeDtypeStruct((1, 1), F32)),
-        in_specs=[in_vmem] * 5,
+        in_specs=[pl.BlockSpec(memory_space=pl.ANY)] * 5,
         out_specs=(in_vmem,) * 6,
-        compiler_params=pltpu.CompilerParams(vmem_limit_bytes=16 * 1024 * 1024),
+        scratch_shapes=[
+            pltpu.VMEM((TABLE_ROWS, tile), F32),
+            pltpu.SemaphoreType.DMA((5,)),
+        ],
+        compiler_params=pltpu.CompilerParams(vmem_limit_bytes=60 * 1024 * 1024),
         name="hand_out",
     )(*outs)
     return objective.reshape(1), grad_msg, grad_self, grad_dec, grad_head.reshape(dec), grad_input

time: 64.5 us -> 60.5 us (0.938)
  local copies, waits for them, and re-layouts: 3.99 us -> 0 us
    unnamed x10 -> x0, local copies, waits for them, and re-layouts: 3.99 us -> none
    pallas_call x1, Pallas kernels: 0.86 us -> 1.91 us  [shards(): pl.pallas_call(hand_out, out_shape=(*big, jax.ShapeDtypeStruct((1, dec),...]
    pallas_call x1, Pallas kernels: 58 us -> 57.2 us  [shards(): pl.pallas_call(functools.partial(step, n), out_shape=(jax.ShapeDtypeStruc...]
where the time goes in v3:
time: 60.5 us; the launch traced here: 60.4 us
  Pallas kernels  59.1 us (98%)
  between operations  1.29 us (2%)
    pallas_call x1, Pallas kernels, shards(): pl.pallas_call(functools.partial(step, n), out_shape=(jax.ShapeDtypeStruc...  57.2 us
    pallas_call x1, Pallas kernels, shards(): pl.pallas_call(hand_out, out_shape=(*big, jax.ShapeDtypeStruct((1, dec),...  1.91 us

profile of v3, /device:TPU:0, one launch (start us, length us, event | category | flops | bytes accessed | tf_op | source)
XLA Modules:
  0.0 60.4 jit_solution(15311666285651745683)
XLA Ops:
  1.3 57.2 %ranker_step.1 = (f32[512,256]{1,0:T(8,128)}, f32[3,16,256]{2,1,0:T(8,128)}, f32[3,16,256]{2,1,0:T(8,128)}, f32[16,128]{1,0:T(8,128)}, f32[8,128]{1,0:T(8,128)}) custom-call(s32[16]{0:T(128)} %tile_rows.1, s32[16]{0:T(128)} %tile_cols.1, s32[1]{0:T(128)S(6)} %copy.17.tile_live, bf16[512,256]{1,0:T(8,128)(2,1)} %feat.1, bf16[16,128,128]{2,1,0:T(8,128)(2,1)} %vals_in.1, ...), custom_call_target="tpu_custom_call" | custom-call | tf_op jit(solution)/shard_map/ranker_step/pallas_call | solution.py:468
  58.5 1.9 %hand_out.1 = (f32[512,256]{1,0:T(8,128)}, f32[3,16,256]{2,1,0:T(8,128)}, f32[3,16,256]{2,1,0:T(8,128)}, f32[16,128]{1,0:T(8,128)}, f32[1,128]{1,0:T(1,128)}, /*index=5*/f32[1,1]{1,0:T(1,128)}) custom-call(f32[512,256]{1,0:T(8,128)} %get-tuple-element.17.refs_0_, f32[3,16,256]{2,1,0:T(8,128)} %get-tuple-element.18.refs_1_, ...), custom_call_target="tpu_custom_call" | custom-call | tf_op jit(solution)/shard_map/hand_out/pallas_call | solution.py:541

commit v4 on v3

--- a/solution.py
+++ b/solution.py
@@ -368,21 +368,23 @@
         grad_msg[layer] = total[0]
         grad_self[layer] = total[1]
 
+    def open_half(layer, side):
+        rows = half_rows(side)
+        inv = inverse[layer, rows]
+        upd = update[layer, rows]
+        carry = carried[rows]
+        along = jnp.sum(carry * upd, axis=-1, keepdims=True) * (1.0 / width)
+        d_upd = inv * carry - upd * (inv * inv * inv * along)
+        d_update[rows] = d_upd
+        mix = (d_upd * slope[layer, rows]).astype(BF16)
+        d_mixed[rows] = mix
+        d_message[layer, rows] = dot_nt(mix, w_msg[layer]).astype(BF16)
+        send_halves(d_message.at[layer], d_halo.at[layer], 3 + layer, side)
+
+    for side in order[::-1]:
+        open_half(LAYERS - 1, side)
+    dec_term = dot_tn(pooled[...], d_pre)
     for layer in reversed(range(LAYERS)):
-        if layer == LAYERS - 1:
-            dec_term = dot_tn(pooled[...], d_pre)
-        for side in order[::-1]:
-            rows = half_rows(side)
-            inv = inverse[layer, rows]
-            upd = update[layer, rows]
-            carry = carried[rows]
-            along = jnp.sum(carry * upd, axis=-1, keepdims=True) * (1.0 / width)
-            d_upd = inv * carry - upd * (inv * inv * inv * along)
-            d_update[rows] = d_upd
-            mix = (d_upd * slope[layer, rows]).astype(BF16)
-            d_mixed[rows] = mix
-            d_message[layer, rows] = dot_nt(mix, w_msg[layer]).astype(BF16)
-            send_halves(d_message.at[layer], d_halo.at[layer], 3 + layer, side)
         if layer == LAYERS - 1:
             for j in range(n):
                 dec_part[j] = dec_term[j * rows_out : (j + 1) * rows_out].astype(dec_part.dtype)
@@ -414,6 +416,8 @@
             near_arrival(d_halo.at[layer, side], 3 + layer, side).wait_recv()
             term = dot_tn(rim[side], d_halo[layer, side])
             result[rows] = d_update[rows] + term
+            if layer > 0:
+                open_half(layer - 1, side)
     weight_sums(1)
     weight_sums(0)
     for copy in sent:

time: 60.5 us -> 60.3 us (level)
  no operation moved by 1% of the time
where the time goes in v4:
time: 60.3 us; the launch traced here: 60.2 us
  Pallas kernels  58.9 us (98%)
  between operations  1.29 us (2%)
    pallas_call x1, Pallas kernels, shards(): pl.pallas_call(functools.partial(step, n), out_shape=(jax.ShapeDtypeStruc...  57 us
    pallas_call x1, Pallas kernels, shards(): pl.pallas_call(hand_out, out_shape=(*big, jax.ShapeDtypeStruct((1, dec),...  1.91 us

profile of v4, /device:TPU:0, one launch (start us, length us, event | category | flops | bytes accessed | tf_op | source)
XLA Modules:
  0.0 60.2 jit_solution(5989503958459959929)
XLA Ops:
  1.3 57.0 %ranker_step.1 = (f32[512,256]{1,0:T(8,128)}, f32[3,16,256]{2,1,0:T(8,128)}, f32[3,16,256]{2,1,0:T(8,128)}, f32[16,128]{1,0:T(8,128)}, f32[8,128]{1,0:T(8,128)}) custom-call(s32[16]{0:T(128)} %tile_rows.1, s32[16]{0:T(128)} %tile_cols.1, s32[1]{0:T(128)S(6)} %copy.17.tile_live, bf16[512,256]{1,0:T(8,128)(2,1)} %feat.1, bf16[16,128,128]{2,1,0:T(8,128)(2,1)} %vals_in.1, ...), custom_call_target="tpu_custom_call" | custom-call | tf_op jit(solution)/shard_map/ranker_step/pallas_call | solution.py:472
  58.3 1.9 %hand_out.1 = (f32[512,256]{1,0:T(8,128)}, f32[3,16,256]{2,1,0:T(8,128)}, f32[3,16,256]{2,1,0:T(8,128)}, f32[16,128]{1,0:T(8,128)}, f32[1,128]{1,0:T(1,128)}, /*index=5*/f32[1,1]{1,0:T(1,128)}) custom-call(f32[512,256]{1,0:T(8,128)} %get-tuple-element.17.refs_0_, f32[3,16,256]{2,1,0:T(8,128)} %get-tuple-element.18.refs_1_, ...), custom_call_target="tpu_custom_call" | custom-call | tf_op jit(solution)/shard_map/hand_out/pallas_call | solution.py:545
